TPU v7x, 512 devices: a whole 4x4x16 slice. The times are simulated.
512 devices in a mesh: gal: 64 (over z, y_lo, core), qry: 8 (over x, y_hi).
Axes of the slice: x: 4, y: 4 (y_hi: 2, y_lo: 2; y = y_hi * 2 + y_lo), z: 16, core: 2. Of those that a mesh axis runs over, the one named last changes fastest.
Arguments:
- gallery: bfloat16 [262144, 768], P('gal'), may hold values from -24 to 24
- bank: bfloat16 [4096, 768], P('qry'), may hold values from -24 to 24
- test: bfloat16 [2048, 768], P('qry'), may hold values from -24 to 24
Outputs:
- normalizers: float32 [262144], P('gal')
- query_lse: float32 [2048], P('qry')
- pooled: float32 [2048, 768], P('qry')
All inputs are finite; a program needn't handle non-finite values.
Results may differ from a plain program's by a relative error of at most 0.0003.
Values sent between devices are 32-bit elements; how exact they have to be, the bound alone decides.
A program may use at most 128 MiB of HBM per device.

v0:
```python
import math

import jax
import jax.numpy as jnp
from jax import lax
from jax.sharding import PartitionSpec as P


def joined(part, axis, combine):
    gathered = jax.tree.map(lambda a: lax.all_gather(a, axis), part)

    def take(source):
        return jax.tree.map(lambda a: lax.dynamic_index_in_dim(a, source, 0, False), gathered)

    return lax.fori_loop(
        1, lax.axis_size(axis), lambda source, state: combine(state, take(source)), take(0)
    )


def join_parts(earlier, later):
    joined_peak = jnp.maximum(earlier[0], later[0])
    joined_total = earlier[1] * jnp.exp(earlier[0] - joined_peak) + later[1] * jnp.exp(
        later[0] - joined_peak
    )
    return (joined_peak, joined_total)


def body(gallery, bank, test):
    score_scale = 5.0 / math.sqrt(gallery.shape[1])
    contract = (((1,), (1,)), ((), ()))
    bank_logits = score_scale * lax.dot_general(
        bank, gallery, contract, preferred_element_type=jnp.float32
    )
    column_peak = jnp.max(bank_logits, axis=0)
    column_total = jnp.sum(jnp.exp(bank_logits - column_peak[None, :]), axis=0)
    merged_peak, merged_total = joined((column_peak, column_total), "qry", join_parts)
    normalizers = merged_peak + jnp.log(merged_total)
    test_logits = (
        score_scale * lax.dot_general(test, gallery, contract, preferred_element_type=jnp.float32)
        - normalizers[None, :]
    )
    block_peak = jnp.max(test_logits, axis=1)
    exp_terms = jnp.exp(test_logits - block_peak[:, None])
    soft_weights = exp_terms.astype(jnp.bfloat16)
    block_totals = jnp.sum(exp_terms, axis=1)
    block_weighted = jnp.dot(soft_weights, gallery, preferred_element_type=jnp.float32)
    row_max = lax.pmax(block_peak, "gal")
    rescale = jnp.exp(block_peak - row_max)
    scaled_totals = rescale * block_totals
    scaled_weighted = rescale[:, None] * block_weighted
    totals, weighted = lax.psum((scaled_totals, scaled_weighted), "gal")
    pooled = weighted / totals[:, None]
    query_lse = row_max + jnp.log(totals)
    return (normalizers, query_lse, pooled)


def solution(mesh):
    placed = (P("gal", None), P("qry", None), P("qry", None))
    return jax.shard_map(
        body,
        mesh=mesh,
        in_specs=placed,
        out_specs=(P("gal"), P("qry"), P("qry", None)),
        check_vma=False,
    )
```

profile of v0, /device:TPU:1, one launch (start us, length us, event | category | flops | bytes accessed | tf_op | source)
XLA Modules:
  0.0 638.7 jit_solution(17997691022088275766)
XLA Ops:
  7.2 0.0 copy-start
  7.2 0.0 all-reduce.2.cloned.1.call-start
  7.2 1.1 copy-done
  8.3 5.6 multiply_reduce_fusion
  13.9 0.0 copy-start.2
  13.9 1.4 exponential_reduce_fusion
  15.3 28.7 %all-gather.1 = f32[32768]{0:T(1024)S(1)} all-gather(f32[4096]{0:T(1024)S(1)} %exponential_reduce_fusion), channel_id=3, replica_groups=mesh['gal'=64,'qry'=8] {'qry'}, dimensions={0}, use_global_device_ids=true | all-gather | bytes 147456 | tf_op jit(solution)/shard_map/all_gather | solution.py:10
  44.1 27.9 %all-gather = f32[32768]{0:T(1024)S(1)} all-gather(f32[4096]{0:T(1024)S(1)} %get-tuple-element.154), channel_id=2, replica_groups=mesh['gal'=64,'qry'=8] {'qry'}, dimensions={0}, use_global_device_ids=true | all-gather | bytes 147456 | tf_op jit(solution)/shard_map/all_gather | solution.py:10
  72.0 0.6 while.17
  72.6 0.0 copy-done.2
  72.6 0.0 copy-start.1
  72.6 6.6 %fusion.10 = (f32[256]{0:T(256)S(1)}, f32[256,4096]{1,0:T(8,128)}) fusion(f32[4096]{0:T(1024)S(1)} %log_add_fusion, bf16[256,768]{1,0:T(8,128)(2,1)S(1)} %copy-done.2, bf16[4096,768]{1,0:T(8,128)(2,1)} %param.5), kind=kOutput, calls=%fused_computation.18 | convolution fusion | flops 1613758208 | bytes 10896384 | tf_op jit(solution)/shard_map/dot_general | solution.py:39
  79.2 0.0 copy-done.1
  79.2 124.2 %pmax.7 = f32[256]{0:T(256)S(1)} all-reduce(f32[256]{0:T(256)S(1)} %get-tuple-element.156), channel_id=1, replica_groups=mesh['gal'=64,'qry'=8] {'gal'}, use_global_device_ids=true, to_apply=%region_5.6 | all-reduce | flops 256 | bytes 2048 | tf_op jit(solution)/shard_map/pmax | solution.py:47
  203.3 2.9 fusion.2
  206.2 6.8 %fusion.6 = f32[256,768]{1,0:T(8,128)} fusion(bf16[4096,768]{1,0:T(8,128)(2,1)} %param.5, f32[256,4096]{1,0:T(8,128)} %get-tuple-element.157, f32[256]{0:T(256)S(1)} %get-tuple-element.156, f32[256]{0:T(256)S(1)} %get-tuple-element.151), kind=kOutput, calls=%fused_computation.12 | convolution fusion | flops 1612906496 | bytes 11274240 | tf_op jit(solution)/shard_map/dot_general | solution.py:46
  213.0 0.0 all-reduce.2.cloned.1.call-update
  213.1 104.3 %psum.14 = f32[256]{0:T(256)S(1)} all-reduce(f32[256]{0:T(256)S(1)} %get-tuple-element.150), channel_id=1, replica_groups=mesh['gal'=64,'qry'=8] {'gal'}, use_global_device_ids=true, to_apply=%region_7.8 | all-reduce | flops 256 | bytes 2048 | tf_op jit(solution)/shard_map/psum | solution.py:51
  317.4 0.6 log_add_fusion.1
  317.9 311.7 %all-reduce.2.cloned.1.call-done = f32[256,768]{1,0:T(8,128)} async-done(((f32[256,768]{1,0:T(8,128)}), f32[256,768]{1,0:T(8,128)}) %all-reduce.2.cloned.1.call-update) | async-done | bytes 786448 | tf_op jit(solution)/shard_map/psum | solution.py:51
  629.7 2.1 broadcast_divide_fusion
  (20 shorter events, 0.4 us)
Async XLA Ops:
  7.2 1.1 copy-start
  7.2 622.5 %all-reduce.2.cloned.1.call-start = ((), (), s32[]{:S(2)}) async-start(), calls=%async_computation | async-start | bytes 1572864 | tf_op jit(solution)/shard_map/psum | solution.py:51
  13.9 58.7 %copy-start.2 = (bf16[256,768]{1,0:T(8,128)(2,1)S(1)}, bf16[256,768]{1,0:T(8,128)(2,1)}, u32[]{:S(2)}) copy-start(bf16[256,768]{1,0:T(8,128)(2,1)} %param.7) | copy-start | bytes 1179652
  72.6 6.6 %copy-start.1 = (f32[4096]{0:T(1024)}, f32[4096]{0:T(1024)S(1)}, u32[]{:S(2)}) copy-start(f32[4096]{0:T(1024)S(1)} %log_add_fusion) | copy-start | bytes 49156
Sparse Core Ops, SparseCore 0:
  213.2 416.4 all-reduce.1
where the time goes:
time: 639 us
  waiting for transfers between devices  312 us (49%)
  blocking collectives  285 us (45%)
  matrix products  19 us (3%)
  between operations  14.1 us (2%)
  other arithmetic  7.17 us (1%)
    psum x1, waiting for transfers between devices, body(): totals, weighted = lax.psum((scaled_totals, scaled_weighted), 'gal')  312 us
    pmax x1, blocking collectives, body(): row_max = lax.pmax(block_peak, 'gal')  124 us
    psum x1, blocking collectives, body(): totals, weighted = lax.psum((scaled_totals, scaled_weighted), 'gal')  104 us
    all_gather x2, blocking collectives, joined(): gathered = jax.tree.map(lambda a: lax.all_gather(a, axis), part)  56.6 us
  transfers between devices with their start and end apart: 1, of which 1 were waited for; matrix products, arithmetic and copies ran while one was open for 0% of the time, Pallas kernels for 0%

commit v1 on v0

v1 whole, which is shorter than its diff:
```python
import functools
import math

import jax
import jax.numpy as jnp
from jax import lax
from jax.experimental import pallas as pl
from jax.experimental.pallas import tpu as pltpu
from jax.sharding import PartitionSpec as P

MESH = pl.DeviceIdType.MESH
F32 = jnp.float32
BF16 = jnp.bfloat16
LOG2E = math.log2(math.e)
LN2 = math.log(2.0)
NT = (((1,), (1,)), ((), ()))
CLIPS, BANKQ, TESTQ, D = 4096, 512, 256, 768
PARTS = 4
PC = CLIPS // PARTS
PR = PC // 128
FAR = (4, 3, 5, 2, 6, 1, 7)


def kernel(
    gallery, bank, test, norm_out, lse_out, pooled_out,
    gal, bnk, tst, raw, wts, nloc, nrecv, n2, work, crecv, csum, s1recv, s1sum, s2recv, final,
    sc0, sc0r, sc1, sc1r, sc2, sc2r, lsef, e0, e1, e2,
    lsem, osem, nsem, rsem, nsend, ssem,
):
    me, q = lax.axis_index("gal"), lax.axis_index("qry")
    z, y, c = me // 4, (me // 2) % 2, me % 2
    zp, h = z % 2, z // 2
    g = y * 2 + zp

    def at(z_, y_, c_):
        return {"gal": z_ * 4 + y_ * 2 + c_}

    sib = at(z, y, 1 - c)
    zf, yf = z + 1 - 2 * zp, 1 - y
    quad = {
        1: (at(zf, y, c), y * 2 + 1 - zp),
        2: (at(z, yf, c), yf * 2 + zp),
        3: (at(zf, yf, c), yf * 2 + 1 - zp),
    }
    ring = {d: (at(((h + d) % 8) * 2 + zp, y, c), (h + d) % 8) for d in range(1, 8)}
    panel = {d: {"qry": (q + d) % 8} for d in range(1, 8)}

    loads = [pltpu.make_async_copy(bank, bnk, lsem.at[PARTS])]
    for j in range(PARTS):
        rows = pl.ds(j * PC, PC)
        loads.append(pltpu.make_async_copy(gallery.at[rows], gal.at[rows], lsem.at[j]))
    loads.append(pltpu.make_async_copy(test, tst, lsem.at[PARTS + 1]))
    for load in loads:
        load.start()

    barrier = pltpu.get_barrier_semaphore()
    peers = [sib] + [p for p, _ in quad.values()] + [p for p, _ in ring.values()] + list(panel.values())
    for p in peers:
        pl.semaphore_signal(barrier, inc=1, device_id=p, device_id_type=MESH)

    def send(src, dst, stage, k, device):
        pltpu.make_async_remote_copy(
            src_ref=src, dst_ref=dst, send_sem=ssem.at[stage, k], recv_sem=rsem.at[stage, k],
            device_id=device, device_id_type=MESH,
        ).start()

    def arrived(ref, stage, k):
        pltpu.make_async_copy(ref, ref, rsem.at[stage, k]).wait()

    c2 = 5.0 / math.sqrt(D) * LOG2E
    loads[0].wait()

    def bank_part(j, carry):
        rows = pl.ds(pl.multiple_of(j * PC, PC), PC)
        pltpu.make_async_copy(gallery.at[rows], gal.at[rows], lsem.at[j]).wait()
        r = lax.dot_general(bnk[...], gal[rows, :], NT, preferred_element_type=F32)
        m = jnp.max(r, axis=0, keepdims=True)
        s = jnp.sum(jnp.exp2((r - m) * c2), axis=0, keepdims=True)
        l2 = m * c2 + jnp.log(s) * LOG2E
        for i in range(PR):
            nloc[pl.ds(j * PR + i, 1), :] = l2[:, i * 128 : (i + 1) * 128]

        @pl.when(j == 0)
        def _():
            pl.semaphore_wait(barrier, len(peers))

        block = pl.ds(pl.multiple_of(j * PR, PR), PR)
        for d in FAR:
            pltpu.make_async_remote_copy(
                src_ref=nloc.at[block], dst_ref=nrecv.at[d - 1, block],
                send_sem=nsend.at[j], recv_sem=nsem.at[j],
                device_id=panel[d], device_id_type=MESH,
            ).start()
        return carry

    lax.fori_loop(0, PARTS, bank_part, 0)

    loads[-1].wait()

    def test_part(j, carry):
        rows = pl.ds(pl.multiple_of(j * 1024, 1024), 1024)
        raw[:, rows] = lax.dot_general(tst[...], gal[rows, :], NT, preferred_element_type=F32)
        return carry

    lax.fori_loop(0, CLIPS // 1024, test_part, 0)

    def norm_part(j, peak):
        block = pl.ds(pl.multiple_of(j * PR, PR), PR)
        part = nrecv.at[:, block]
        pltpu.make_async_copy(part, part, nsem.at[j]).wait()
        own = nloc[block, :]
        m = own
        for d in range(7):
            m = jnp.maximum(m, nrecv[d, block, :])
        s = jnp.exp2(own - m)
        for d in range(7):
            s = s + jnp.exp2(nrecv[d, block, :] - m)
        n2[block, :] = m + jnp.log(s) * LOG2E

        def shift(i, peak):
            lanes = pl.ds(pl.multiple_of((j * PR + i) * 128, 128), 128)
            x = raw[:, lanes] * c2 - n2[pl.ds(j * PR + i, 1), :]
            raw[:, lanes] = x
            return jnp.maximum(peak, x)

        return lax.fori_loop(0, PR, shift, peak, unroll=2)

    peak = lax.fori_loop(0, PARTS, norm_part, jnp.full((TESTQ, 128), -jnp.inf, F32))
    peak = jnp.max(peak, axis=1, keepdims=True)
    norm_out[...] = n2[...] * LN2

    def weigh(i, total):
        lanes = pl.ds(pl.multiple_of(i * 128, 128), 128)
        e = jnp.exp2(raw[:, lanes] - peak)
        wts[:, lanes] = e.astype(BF16)
        return total + e

    total = lax.fori_loop(0, CLIPS // 128, weigh, jnp.zeros((TESTQ, 128), F32), unroll=2)
    total = jnp.sum(total, axis=1, keepdims=True)

    def packed(m, t):
        lane = lax.broadcasted_iota(jnp.int32, m.shape, 1)
        return jnp.where(lane < 64, m, t)

    def spread(a, lane):
        return jnp.broadcast_to(a[:, lane : lane + 1], a.shape)

    def merged(tiles, scales):
        ms, ts = [spread(a, 0) for a in tiles], [spread(a, 64) for a in tiles]
        m = functools.reduce(jnp.maximum, ms)
        t = None
        for i, (mi, ti) in enumerate(zip(ms, ts)):
            e = jnp.exp2(mi - m)
            scales[i] = e
            t = e * ti if t is None else t + e * ti
        return m, t

    sc0[...] = packed(jnp.broadcast_to(peak, (TESTQ, 128)), jnp.broadcast_to(total, (TESTQ, 128)))
    send(sc0, sc0r, 0, 3, sib)

    def pool(tile):
        lanes = pl.ds(pl.multiple_of(tile * 256, 256), 256)
        out = jnp.dot(wts[...], gal[:, lanes], preferred_element_type=F32)
        work[2 * tile] = out[:, :128]
        work[2 * tile + 1] = out[:, 128:]

    pool(2 * (1 - c))
    send(work.at[pl.ds(4 * (1 - c), 2)], crecv.at[pl.ds(1, 2)], 0, 1, sib)
    arrived(sc0r, 0, 3)
    m, t = merged([sc0[...], sc0r[...]], e0)
    sc1[...] = packed(m, t)
    for r in (3, 1, 2):
        device, gp = quad[r]
        send(sc1.at[pl.ds(gp * 64, 64)], sc1r.at[r - 1], 1, 3, device)
    pool(1)
    send(work.at[3 - c], crecv.at[0], 0, 0, sib)
    pool(2 * c)

    own = (2 + c, 4 * c, 4 * c + 1)
    for k in range(3):
        if k == 0:
            arrived(crecv.at[0], 0, 0)
        if k == 1:
            arrived(crecv.at[pl.ds(1, 2)], 0, 1)
        csum[k] = e0[0] * work[own[k]] + e0[1] * crecv[k]
        for r in (3, 1, 2):
            device, gp = quad[r]
            send(csum.at[k, pl.ds(gp * 64, 64)], s1recv.at[r - 1, k], 1, k, device)

    rows64 = pl.ds(pl.multiple_of(g * 64, 64), 64)
    rows8 = pl.ds(pl.multiple_of(h * 8, 8), 8)
    rows = pl.ds(pl.multiple_of(g * 64 + h * 8, 8), 8)
    arrived(sc1r, 1, 3)
    m, t = merged([sc1[rows64, :]] + [sc1r[i] for i in range(3)], e1)
    sc2[...] = packed(m, t)
    for d in FAR:
        device, hp = ring[d]
        send(sc2.at[pl.ds(hp * 8, 8)], sc2r.at[d - 1], 2, 3, device)

    for k in range(3):
        arrived(s1recv.at[:, k], 1, k)
        acc = e1[0] * csum[k, rows64, :]
        for i in range(3):
            acc = acc + e1[i + 1] * s1recv[i, k]
        s1sum[k] = acc
        for d in FAR:
            device, hp = ring[d]
            send(s1sum.at[k, pl.ds(hp * 8, 8)], s2recv.at[d - 1, k], 2, k, device)

    arrived(sc2r, 2, 3)
    m, t = merged([sc2[rows8, :]] + [sc2r[i] for i in range(7)], e2)
    lsef[rows, :] = m * LN2 + jnp.log(t)
    for d in FAR:
        send(lsef.at[rows], lsef.at[rows], 3, 3, ring[d][0])
    inv = 1.0 / t
    for k in range(3):
        arrived(s2recv.at[:, k], 2, k)
        acc = e2[0] * s1sum[k, rows8, :]
        for i in range(7):
            acc = acc + e2[i + 1] * s2recv[i, k]
        final[own[k], rows, :] = acc * inv
        for d in FAR:
            send(final.at[own[k], rows], final.at[own[k], rows], 3, k, ring[d][0])

    arrived(sc2r, 3, 3)
    for r in (3, 1, 2):
        send(lsef.at[rows64], lsef.at[rows64], 4, 3, quad[r][0])
    for k in range(3):
        arrived(s2recv.at[:, k], 3, k)
        for r in (3, 1, 2):
            send(final.at[own[k], rows64], final.at[own[k], rows64], 4, k, quad[r][0])

    arrived(sc1r, 4, 3)
    sub = lax.broadcasted_iota(jnp.int32, (128, 128), 0)
    lane = lax.broadcasted_iota(jnp.int32, (128, 128), 1)
    for i in range(2):
        tile = lsef[i * 128 : (i + 1) * 128, :]
        lse_out[i : i + 1, :] = jnp.sum(jnp.where(sub == lane, tile, 0.0), axis=0, keepdims=True)

    def store(b, k):
        return pltpu.make_async_copy(
            final.at[b], pooled_out.at[:, pl.ds(pl.multiple_of(b * 128, 128), 128)], osem.at[k]
        )

    for k in range(3):
        arrived(s1recv.at[:, k], 4, k)
        send(final.at[own[k]], final.at[own[k]], 5, k, sib)
        store(own[k], k).start()
    other = (3 - c, 4 * (1 - c), 4 * (1 - c) + 1)
    for k in range(3):
        arrived(crecv.at[k], 5, k)
        store(other[k], 3 + k).start()
    for k in range(3):
        store(own[k], k).wait()
        store(other[k], 3 + k).wait()

    def sent(ref, stage, k):
        pltpu.make_async_copy(ref, ref, ssem.at[stage, k]).wait()

    for j in range(PARTS):
        part = nrecv.at[:, j * PR : (j + 1) * PR]
        pltpu.make_async_copy(part, part, nsend.at[j]).wait()
    sent(sc0r, 0, 3)
    sent(crecv.at[pl.ds(1, 2)], 0, 1)
    sent(crecv.at[0], 0, 0)
    sent(sc1r, 1, 3)
    sent(sc2r, 2, 3)
    sent(sc2r, 3, 3)
    sent(sc1r, 4, 3)
    for k in range(3):
        sent(s1recv.at[:, k], 1, k)
        sent(s2recv.at[:, k], 2, k)
        sent(s2recv.at[:, k], 3, k)
        sent(s1recv.at[:, k], 4, k)
        sent(crecv.at[k], 5, k)


def body(gallery, bank, test):
    vm = pltpu.VMEM
    dma = pltpu.SemaphoreType.DMA
    norm, lse, pooled = pl.pallas_call(
        kernel,
        out_shape=(
            jax.ShapeDtypeStruct((CLIPS // 128, 128), F32),
            jax.ShapeDtypeStruct((TESTQ // 128, 128), F32),
            jax.ShapeDtypeStruct((TESTQ, D), F32),
        ),
        in_specs=[pl.BlockSpec(memory_space=pl.ANY)] * 3,
        out_specs=(
            pl.BlockSpec(memory_space=pltpu.VMEM),
            pl.BlockSpec(memory_space=pltpu.VMEM),
            pl.BlockSpec(memory_space=pl.ANY),
        ),
        scratch_shapes=[
            vm((CLIPS, D), BF16),
            vm((BANKQ, D), BF16),
            vm((TESTQ, D), BF16),
            vm((TESTQ, CLIPS), F32),
            vm((TESTQ, CLIPS), BF16),
            vm((CLIPS // 128, 128), F32),
            vm((7, CLIPS // 128, 128), F32),
            vm((CLIPS // 128, 128), F32),
            vm((6, TESTQ, 128), F32),
            vm((3, TESTQ, 128), F32),
            vm((3, TESTQ, 128), F32),
            vm((3, 3, 64, 128), F32),
            vm((3, 64, 128), F32),
            vm((7, 3, 8, 128), F32),
            vm((6, TESTQ, 128), F32),
            vm((TESTQ, 128), F32),
            vm((TESTQ, 128), F32),
            vm((TESTQ, 128), F32),
            vm((3, 64, 128), F32),
            vm((64, 128), F32),
            vm((7, 8, 128), F32),
            vm((TESTQ, 128), F32),
            vm((2, TESTQ, 128), F32),
            vm((4, 64, 128), F32),
            vm((8, 8, 128), F32),
            dma((PARTS + 2,)),
            dma((6,)),
            dma((PARTS,)),
            dma((6, 4)),
            dma((PARTS,)),
            dma((6, 4)),
        ],
        compiler_params=pltpu.CompilerParams(
            collective_id=0, has_side_effects=True, vmem_limit_bytes=48 * 2**20
        ),
    )(gallery, bank, test)
    return norm.reshape(CLIPS), lse.reshape(TESTQ), pooled


def solution(mesh):
    placed = (P("gal", None), P("qry", None), P("qry", None))
    return jax.shard_map(
        body,
        mesh=mesh,
        in_specs=placed,
        out_specs=(P("gal"), P("qry"), P("qry", None)),
        check_vma=False,
    )
```

time: 639 us -> 66.1 us (0.10)
  waiting for transfers between devices: 312 us -> 0 us
  blocking collectives: 285 us -> 0 us
  Pallas kernels: 0 us -> 61.1 us
  matrix products: 19 us -> 0 us
  between operations: 14.1 us -> 0.65 us
  other arithmetic: 7.17 us -> 0 us
    psum x1 -> x0, waiting for transfers between devices: 312 us -> none  [body(): totals, weighted = lax.psum((scaled_totals, scaled_weighted), 'gal')]
    pmax x1 -> x0, blocking collectives: 124 us -> none  [body(): row_max = lax.pmax(block_peak, 'gal')]
    psum x1 -> x0, blocking collectives: 104 us -> none  [body(): totals, weighted = lax.psum((scaled_totals, scaled_weighted), 'gal')]
    pallas_call x0 -> x1, Pallas kernels: none -> 61.1 us  [body(): pl.pallas_call(kernel, out_shape=(jax.ShapeDtypeStruct((CLIPS // 128, 128...]
    all_gather x2 -> x0, blocking collectives: 56.6 us -> none  [joined(): gathered = jax.tree.map(lambda a: lax.all_gather(a, axis), part)]
    dot_general x3 -> x0, matrix products: 19 us -> none  [the longest x1 6.8 us: body(): jnp.dot(soft_weights, gallery, preferred_element_type=jnp.float32)]
  transfers between devices with their start and end apart: 1 -> 0, of which waited for: 1 -> 0; matrix products, arithmetic and copies ran while one was open for 0% -> 0% of each run, Pallas kernels for 0% -> 0%
where the time goes in v1:
time: 66.1 us; the launch traced here: 65.9 us
  Pallas kernels  61.1 us (92%)
  local copies, waits for them, and re-layouts  4.17 us (6%)
    pallas_call x1, Pallas kernels, body(): pl.pallas_call(kernel, out_shape=(jax.ShapeDtypeStruct((CLIPS // 128, 128...  61.1 us
    unnamed x7, local copies, waits for them, and re-layouts  4.17 us

profile of v1, /device:TPU:1, one launch (start us, length us, event | category | flops | bytes accessed | tf_op | source)
XLA Modules:
  0.0 65.9 jit_solution(13041525961040185681)
XLA Ops:
  0.6 0.0 copy-start
  0.6 1.1 %copy-done = bf16[512,768]{1,0:T(8,128)(2,1)S(1)} copy-done((bf16[512,768]{1,0:T(8,128)(2,1)S(1)}, bf16[512,768]{1,0:T(8,128)(2,1)}, u32[]{:S(2)}) %copy-start) | copy-done | bytes 786456
  1.8 0.0 copy-start.1
  1.8 1.0 %copy-done.1 = bf16[256,768]{1,0:T(8,128)(2,1)S(1)} copy-done((bf16[256,768]{1,0:T(8,128)(2,1)S(1)}, bf16[256,768]{1,0:T(8,128)(2,1)}, u32[]{:S(2)}) %copy-start.1) | copy-done | bytes 393240
  2.8 61.1 %shard_map.58 = (f32[32,128]{1,0:T(8,128)S(1)}, f32[2,128]{1,0:T(2,128)S(1)}, f32[256,768]{1,0:T(8,128)S(1)}) custom-call(bf16[4096,768]{1,0:T(8,128)(2,1)} %gallery.1, bf16[512,768]{1,0:T(8,128)(2,1)S(1)} %copy-done, bf16[256,768]{1,0:T(8,128)(2,1)S(1)} %copy-done.1), custom_call_target="tpu_custom_call" | custom-call | tf_op jit(solution)/shard_map/pallas_call | solution.py:281
  63.9 0.6 copy.9
  64.5 0.6 copy.10
  65.1 0.9 %copy.11 = f32[256,768]{1,0:T(8,128)} copy(f32[256,768]{1,0:T(8,128)S(1)} %get-tuple-element.14) | data formatting | bytes 1572864
Async XLA Ops:
  0.6 1.1 %copy-start = (bf16[512,768]{1,0:T(8,128)(2,1)S(1)}, bf16[512,768]{1,0:T(8,128)(2,1)}, u32[]{:S(2)}) copy-start(bf16[512,768]{1,0:T(8,128)(2,1)} %bank.1) | copy-start | bytes 2359300
  1.8 1.0 %copy-start.1 = (bf16[256,768]{1,0:T(8,128)(2,1)S(1)}, bf16[256,768]{1,0:T(8,128)(2,1)}, u32[]{:S(2)}) copy-start(bf16[256,768]{1,0:T(8,128)(2,1)} %test.1) | copy-start | bytes 1179652

commit v2 on v1

v2 whole, which is shorter than its diff:
```python
import functools
import math

import jax
import jax.numpy as jnp
from jax import lax
from jax.experimental import pallas as pl
from jax.experimental.pallas import tpu as pltpu
from jax.sharding import PartitionSpec as P

MESH = pl.DeviceIdType.MESH
F32 = jnp.float32
BF16 = jnp.bfloat16
LOG2E = math.log2(math.e)
LN2 = math.log(2.0)
NT = (((1,), (1,)), ((), ()))
CLIPS, BANKQ, TESTQ, D = 4096, 512, 256, 768
PARTS = 4
PC = CLIPS // PARTS
PR = PC // 128
SPAN = (pl.ds(0, CLIPS // 128 - PR), pl.ds(CLIPS // 128 - PR, PR))
FAR = (4, 3, 5, 2, 6, 1, 7)
NEAR = (0, 1, 7, 2, 6, 3, 5, 4)
QUAD_IN, RING_OUT, QUAD_OUT = 9, 17, 25


def kernel(
    gallery, bank, test, norm_out, lse_out, pooled_out,
    gal, bnk, tst, raw, wts, nloc, nrecv, n2, work, crecv, csum, s1recv, s1sum, s2recv, final,
    sc0, sc0r, sc1, sc1r, sc2, sc2r, lsef, e0, e1, e2,
    lsem, osem, nsem, rsem, nsend, ssem,
):
    me, q = lax.axis_index("gal"), lax.axis_index("qry")
    z, y, c = me // 4, (me // 2) % 2, me % 2
    zp, h = z % 2, z // 2
    g = y * 2 + zp

    def at(z_, y_, c_):
        return {"gal": z_ * 4 + y_ * 2 + c_}

    sib = at(z, y, 1 - c)
    zf, yf = z + 1 - 2 * zp, 1 - y
    quad = {
        1: (at(zf, y, c), y * 2 + 1 - zp),
        2: (at(z, yf, c), yf * 2 + zp),
        3: (at(zf, yf, c), yf * 2 + 1 - zp),
    }
    ring = {d: (at(((h + d) % 8) * 2 + zp, y, c), (h + d) % 8) for d in range(1, 8)}
    panel = {d: {"qry": (q + d) % 8} for d in range(1, 8)}

    loads = [pltpu.make_async_copy(bank, bnk, lsem.at[PARTS])]
    for j in range(PARTS):
        rows = pl.ds(j * PC, PC)
        loads.append(pltpu.make_async_copy(gallery.at[rows], gal.at[rows], lsem.at[j]))
    loads.append(pltpu.make_async_copy(test, tst, lsem.at[PARTS + 1]))
    for load in loads:
        load.start()

    barrier = pltpu.get_barrier_semaphore()
    peers = [sib] + [p for p, _ in quad.values()] + [p for p, _ in ring.values()] + list(panel.values())
    for p in peers:
        pl.semaphore_signal(barrier, inc=1, device_id=p, device_id_type=MESH)

    def send(src, dst, stage, slot, device):
        pltpu.make_async_remote_copy(
            src_ref=src, dst_ref=dst, send_sem=ssem.at[stage], recv_sem=rsem.at[slot],
            device_id=device, device_id_type=MESH,
        ).start()

    def arrived(ref, slot):
        pltpu.make_async_copy(ref, ref, rsem.at[slot]).wait()

    c2 = 5.0 / math.sqrt(D) * LOG2E
    loads[0].wait()

    def bank_part(j, carry):
        rows = pl.ds(pl.multiple_of(j * PC, PC), PC)
        pltpu.make_async_copy(gallery.at[rows], gal.at[rows], lsem.at[j]).wait()
        r = lax.dot_general(bnk[...], gal[rows, :], NT, preferred_element_type=F32)
        m = jnp.max(r, axis=0, keepdims=True)
        s = jnp.sum(jnp.exp2((r - m) * c2), axis=0, keepdims=True)
        l2 = m * c2 + jnp.log(s) * LOG2E
        for i in range(PR):
            nloc[pl.ds(j * PR + i, 1), :] = l2[:, i * 128 : (i + 1) * 128]
        return carry

    def send_part(i):
        for d in FAR:
            pltpu.make_async_remote_copy(
                src_ref=nloc.at[SPAN[i]], dst_ref=nrecv.at[d - 1, SPAN[i]],
                send_sem=nsend.at[i], recv_sem=nsem.at[i],
                device_id=panel[d], device_id_type=MESH,
            ).start()

    lax.fori_loop(0, PARTS - 1, bank_part, 0)
    pl.semaphore_wait(barrier, len(peers))
    send_part(0)
    bank_part(PARTS - 1, 0)
    send_part(1)

    loads[-1].wait()

    def test_part(j, carry):
        rows = pl.ds(pl.multiple_of(j * 1024, 1024), 1024)
        raw[:, rows] = lax.dot_general(tst[...], gal[rows, :], NT, preferred_element_type=F32)
        return carry

    lax.fori_loop(0, CLIPS // 1024, test_part, 0)

    peak = jnp.full((TESTQ, 128), -jnp.inf, F32)
    for i, block in enumerate(SPAN):
        part = nrecv.at[:, block]
        pltpu.make_async_copy(part, part, nsem.at[i]).wait()
        own = nloc[block, :]
        m = own
        for d in range(7):
            m = jnp.maximum(m, nrecv[d, block, :])
        s = jnp.exp2(own - m)
        for d in range(7):
            s = s + jnp.exp2(nrecv[d, block, :] - m)
        n2[block, :] = m + jnp.log(s) * LOG2E

        def shift(i, peak):
            lanes = pl.ds(pl.multiple_of(i * 128, 128), 128)
            x = raw[:, lanes] * c2 - n2[pl.ds(i, 1), :]
            raw[:, lanes] = x
            return jnp.maximum(peak, x)

        peak = lax.fori_loop(block.start, block.start + block.size, shift, peak, unroll=2)
    peak = jnp.max(peak, axis=1, keepdims=True)
    norm_out[...] = n2[...] * LN2

    def weigh(i, total):
        lanes = pl.ds(pl.multiple_of(i * 128, 128), 128)
        e = jnp.exp2(raw[:, lanes] - peak)
        wts[:, lanes] = e.astype(BF16)
        return total + e

    total = lax.fori_loop(0, CLIPS // 128, weigh, jnp.zeros((TESTQ, 128), F32), unroll=2)
    total = jnp.sum(total, axis=1, keepdims=True)

    def packed(m, t):
        lane = lax.broadcasted_iota(jnp.int32, m.shape, 1)
        return jnp.where(lane < 64, m, t)

    def spread(a, lane):
        return jnp.broadcast_to(a[:, lane : lane + 1], a.shape)

    def merged(tiles, scales):
        ms, ts = [spread(a, 0) for a in tiles], [spread(a, 64) for a in tiles]
        m = functools.reduce(jnp.maximum, ms)
        t = None
        for i, (mi, ti) in enumerate(zip(ms, ts)):
            e = jnp.exp2(mi - m)
            scales[i] = e
            t = e * ti if t is None else t + e * ti
        return m, t

    sc0[...] = packed(jnp.broadcast_to(peak, (TESTQ, 128)), jnp.broadcast_to(total, (TESTQ, 128)))
    send(sc0, sc0r, 0, 0, sib)

    def pool(tile):
        lanes = pl.ds(pl.multiple_of(tile * 256, 256), 256)
        out = jnp.dot(wts[...], gal[:, lanes], preferred_element_type=F32)
        work[2 * tile] = out[:, :128]
        work[2 * tile + 1] = out[:, 128:]

    mid, outer = 2 - 2 * c, c
    pool(2 * (1 - c))
    send(work.at[pl.ds(4 * (1 - c), 2)], crecv.at[pl.ds(1 - c, 2)], 1, 1, sib)
    arrived(sc0r, 0)
    m, t = merged([sc0[...], sc0r[...]], e0)
    sc1[...] = packed(m, t)
    for r in (3, 1, 2):
        device, gp = quad[r]
        send(sc1.at[pl.ds(gp * 64, 64)], sc1r.at[r - 1], 2, 3, device)
    pool(1)
    send(work.at[3 - c], crecv.at[2 * c], 1, 2, sib)
    pool(2 * c)

    def core_sum(k, b):
        both = e0[0] * work[b] + e0[1] * crecv[k]
        csum[k] = both.reshape(4, 8, 8, 128)

    arrived(crecv.at[pl.ds(outer, 2)], 1)
    for i in range(2):
        core_sum(outer + i, 4 * c + i)
    arrived(crecv.at[mid], 2)
    core_sum(mid, 2 + c)

    for d in FAR + (0,):
        for r in (3, 1, 2):
            device, gp = quad[r]
            send(csum.at[:, gp, (h + d) % 8], s1recv.at[r - 1, d], 3, QUAD_IN + d, device)

    arrived(sc1r, 3)
    m, t = merged([sc1[pl.ds(pl.multiple_of(g * 64, 64), 64), :]] + [sc1r[i] for i in range(3)], e1)
    sc2[...] = packed(m, t)
    for d in FAR:
        device, hp = ring[d]
        send(sc2.at[pl.ds(hp * 8, 8)], sc2r.at[d - 1], 4, 4, device)

    for d in FAR + (0,):
        hp = (h + d) % 8
        rows = pl.ds(pl.multiple_of(hp * 8, 8), 8)
        arrived(s1recv.at[:, d], QUAD_IN + d)
        acc = e1[0, rows, :] * csum[:, g, hp]
        for i in range(3):
            acc = acc + e1[i + 1, rows, :] * s1recv[i, d]
        s1sum[d] = acc
        if d:
            send(s1sum.at[d], s2recv.at[d - 1], 5, 5, ring[d][0])

    arrived(sc2r, 4)
    rows8 = pl.ds(pl.multiple_of(h * 8, 8), 8)
    m, t = merged([sc2[rows8, :]] + [sc2r[i] for i in range(7)], e2)
    lsef[g, h] = m * LN2 + jnp.log(t)
    for d in FAR:
        send(lsef.at[g, h], lsef.at[g, h], 6, 6, ring[d][0])
    inv = 1.0 / t
    mine = pl.ds(3 * c, 3)
    arrived(s2recv, 5)
    acc = e2[0] * s1sum[0]
    for i in range(7):
        acc = acc + e2[i + 1] * s2recv[i]
    final[mine, g, h] = acc * inv
    for d in FAR:
        send(final.at[mine, g, h], final.at[mine, g, h], 7, RING_OUT + d, ring[d][0])

    for d in NEAR:
        hp = (h - d + 8) % 8
        if d:
            arrived(s2recv.at[0], RING_OUT + d)
        piece = final.at[mine, g, hp]
        for r in (3, 1, 2):
            send(piece, piece, 8, QUAD_OUT + d, quad[r][0])
        if d == 6:
            arrived(sc2r, 6)
            for r in (3, 1, 2):
                send(lsef.at[g], lsef.at[g], 9, 7, quad[r][0])

    for d in NEAR:
        hp = (h - d + 8) % 8
        arrived(s1recv.at[:, 0], QUAD_OUT + d)
        send(final.at[mine, :, hp], final.at[mine, :, hp], 10, 8, sib)

    def store(b, k):
        lanes = pl.ds(pl.multiple_of(b * 128, 128), 128)
        return pltpu.make_async_copy(final.at[b], pooled_out.at[:, :, :, lanes], osem.at[k])

    for k in range(3):
        store(3 * c + k, k).start()
    arrived(sc1r, 7)
    sub = lax.broadcasted_iota(jnp.int32, (128, 128), 0)
    lane = lax.broadcasted_iota(jnp.int32, (128, 128), 1)
    for i in range(2):
        tile = lsef[2 * i : 2 * i + 2].reshape(128, 128)
        lse_out[i : i + 1, :] = jnp.sum(jnp.where(sub == lane, tile, 0.0), axis=0, keepdims=True)
    arrived(crecv, 8)
    for k in range(3):
        store(3 - 3 * c + k, 3 + k).start()
    for k in range(3):
        store(3 * c + k, k).wait()
        store(3 - 3 * c + k, 3 + k).wait()

    for i, block in enumerate(SPAN):
        part = nrecv.at[:, block]
        pltpu.make_async_copy(part, part, nsend.at[i]).wait()
    for stage, ref in enumerate((sc0r, crecv, sc1r, s1recv, sc2r, s2recv, sc2r, s2recv, s1recv, sc1r, crecv)):
        pltpu.make_async_copy(ref, ref, ssem.at[stage]).wait()


def write(norm, lse, pooled, norm_out, lse_out, pooled_out):
    norm_out[...] = norm[...]
    lse_out[...] = lse[...]
    pooled_out[...] = pooled[...]


def body(gallery, bank, test):
    vm = pltpu.VMEM
    dma = pltpu.SemaphoreType.DMA
    norm, lse, pooled = pl.pallas_call(
        kernel,
        out_shape=(
            jax.ShapeDtypeStruct((CLIPS // 128, 128), F32),
            jax.ShapeDtypeStruct((TESTQ // 128, 128), F32),
            jax.ShapeDtypeStruct((4, 8, 8, D), F32),
        ),
        in_specs=[pl.BlockSpec(memory_space=pl.ANY)] * 3,
        out_specs=(
            pl.BlockSpec(memory_space=pltpu.VMEM),
            pl.BlockSpec(memory_space=pltpu.VMEM),
            pl.BlockSpec(memory_space=pl.ANY),
        ),
        scratch_shapes=[
            vm((CLIPS, D), BF16),
            vm((BANKQ, D), BF16),
            vm((TESTQ, D), BF16),
            vm((TESTQ, CLIPS), F32),
            vm((TESTQ, CLIPS), BF16),
            vm((CLIPS // 128, 128), F32),
            vm((7, CLIPS // 128, 128), F32),
            vm((CLIPS // 128, 128), F32),
            vm((6, TESTQ, 128), F32),
            vm((3, TESTQ, 128), F32),
            vm((3, 4, 8, 8, 128), F32),
            vm((3, 8, 3, 8, 128), F32),
            vm((8, 3, 8, 128), F32),
            vm((7, 3, 8, 128), F32),
            vm((6, 4, 8, 8, 128), F32),
            vm((TESTQ, 128), F32),
            vm((TESTQ, 128), F32),
            vm((TESTQ, 128), F32),
            vm((3, 64, 128), F32),
            vm((64, 128), F32),
            vm((7, 8, 128), F32),
            vm((4, 8, 8, 128), F32),
            vm((2, TESTQ, 128), F32),
            vm((4, 64, 128), F32),
            vm((8, 8, 128), F32),
            dma((PARTS + 2,)),
            dma((6,)),
            dma((2,)),
            dma((33,)),
            dma((2,)),
            dma((11,)),
        ],
        compiler_params=pltpu.CompilerParams(
            collective_id=0, has_side_effects=True, vmem_limit_bytes=62 * 2**20
        ),
    )(gallery, bank, test)
    norm, lse, pooled = pl.pallas_call(
        write,
        out_shape=tuple(jax.ShapeDtypeStruct(a.shape, F32) for a in (norm, lse, pooled)),
        in_specs=[pl.BlockSpec(memory_space=pltpu.VMEM)] * 3,
        out_specs=(pl.BlockSpec(memory_space=pltpu.VMEM),) * 3,
    )(norm, lse, pooled)
    return norm.reshape(CLIPS), lse.reshape(TESTQ), pooled.reshape(TESTQ, D)


def solution(mesh):
    placed = (P("gal", None), P("qry", None), P("qry", None))
    return jax.shard_map(
        body,
        mesh=mesh,
        in_specs=placed,
        out_specs=(P("gal"), P("qry"), P("qry", None)),
        check_vma=False,
    )
```

time: 66.1 us -> 62.2 us (0.941)
  local copies, waits for them, and re-layouts: 4.17 us -> 0 us
    unnamed x7 -> x0, local copies, waits for them, and re-layouts: 4.17 us -> none
    pallas_call x0 -> x1, Pallas kernels: none -> 2.09 us  [body(): pl.pallas_call(write, out_shape=tuple((jax.ShapeDtypeStruct(a.shape, F32)...]
    pallas_call x1, Pallas kernels: 61.1 us -> 59.3 us  [body(): pl.pallas_call(kernel, out_shape=(jax.ShapeDtypeStruct((CLIPS // 128, 128...]
where the time goes in v2:
time: 62.2 us; the launch traced here: 62.1 us
  Pallas kernels  61.4 us (99%)
  between operations  0.64 us (1%)
    pallas_call x1, Pallas kernels, body(): pl.pallas_call(kernel, out_shape=(jax.ShapeDtypeStruct((CLIPS // 128, 128...  59.3 us
    pallas_call x1, Pallas kernels, body(): pl.pallas_call(write, out_shape=tuple((jax.ShapeDtypeStruct(a.shape, F32)...  2.09 us

profile of v2, /device:TPU:1, one launch (start us, length us, event | category | flops | bytes accessed | tf_op | source)
XLA Modules:
  0.0 62.1 jit_solution(11964337302404065412)
XLA Ops:
  0.6 59.3 %shard_map.58 = (f32[32,128]{1,0:T(8,128)}, f32[2,128]{1,0:T(2,128)}, f32[4,8,8,768]{3,2,1,0:T(8,128)}) custom-call(bf16[4096,768]{1,0:T(8,128)(2,1)} %gallery.1, bf16[512,768]{1,0:T(8,128)(2,1)} %bank.1, bf16[256,768]{1,0:T(8,128)(2,1)} %test.1), custom_call_target="tpu_custom_call" | custom-call | tf_op jit(solution)/shard_map/pallas_call | solution.py:282
  60.0 2.1 %shard_map.59 = (f32[32,128]{1,0:T(8,128)}, f32[2,128]{1,0:T(2,128)}, f32[4,8,8,768]{3,2,1,0:T(8,128)}) custom-call(f32[32,128]{1,0:T(8,128)} %get-tuple-element.9.norm, f32[2,128]{1,0:T(2,128)} %get-tuple-element.10.lse, f32[4,8,8,768]{3,2,1,0:T(8,128)} %get-tuple-element.11.pooled), custom_call_target="tpu_custom_call" | custom-call | tf_op jit(solution)/shard_map/pallas_call | solution.py:332

commit v3 on v2

--- a/solution.py
+++ b/solution.py
@@ -19,16 +19,14 @@
 PC = CLIPS // PARTS
 PR = PC // 128
 SPAN = (pl.ds(0, CLIPS // 128 - PR), pl.ds(CLIPS // 128 - PR, PR))
-FAR = (4, 3, 5, 2, 6, 1, 7)
-NEAR = (0, 1, 7, 2, 6, 3, 5, 4)
 QUAD_IN, RING_OUT, QUAD_OUT = 9, 17, 25
 
 
 def kernel(
-    gallery, bank, test, norm_out, lse_out, pooled_out,
-    gal, bnk, tst, raw, wts, nloc, nrecv, n2, work, crecv, csum, s1recv, s1sum, s2recv, final,
+    gallery, bank, test, norm_out, lse_out, final,
+    gal, bnk, tst, raw, wts, nloc, nrecv, n2, work, crecv, csum, s1recv, s1sum, s2recv,
     sc0, sc0r, sc1, sc1r, sc2, sc2r, lsef, e0, e1, e2,
-    lsem, osem, nsem, rsem, nsend, ssem,
+    lsem, nsem, rsem, nsend, ssem,
 ):
     me, q = lax.axis_index("gal"), lax.axis_index("qry")
     z, y, c = me // 4, (me // 2) % 2, me % 2
@@ -45,8 +43,22 @@
         2: (at(z, yf, c), yf * 2 + zp),
         3: (at(zf, yf, c), yf * 2 + 1 - zp),
     }
-    ring = {d: (at(((h + d) % 8) * 2 + zp, y, c), (h + d) % 8) for d in range(1, 8)}
-    panel = {d: {"qry": (q + d) % 8} for d in range(1, 8)}
+
+    def ring(d):
+        return at(((h + d) % 8) * 2 + zp, y, c)
+
+    def panel(d):
+        return {"qry": (q + d) % 8}
+
+    def distance(i):
+        return 4 + (i + 1) // 2 * (1 - 2 * (i % 2))
+
+    def each(n, step):
+        def run(i, carry):
+            step(i)
+            return carry
+
+        lax.fori_loop(0, n, run, 0)
 
     loads = [pltpu.make_async_copy(bank, bnk, lsem.at[PARTS])]
     for j in range(PARTS):
@@ -57,9 +69,17 @@
         load.start()
 
     barrier = pltpu.get_barrier_semaphore()
-    peers = [sib] + [p for p, _ in quad.values()] + [p for p, _ in ring.values()] + list(panel.values())
-    for p in peers:
-        pl.semaphore_signal(barrier, inc=1, device_id=p, device_id_type=MESH)
+
+    def greet(device):
+        pl.semaphore_signal(barrier, inc=1, device_id=device, device_id_type=MESH)
+
+    def greet_far(i):
+        greet(ring(distance(i)))
+        greet(panel(distance(i)))
+
+    each(7, greet_far)
+    for device in [sib] + [p for p, _ in quad.values()]:
+        greet(device)
 
     def send(src, dst, stage, slot, device):
         pltpu.make_async_remote_copy(
@@ -72,6 +92,17 @@
 
     c2 = 5.0 / math.sqrt(D) * LOG2E
     loads[0].wait()
+
+    def send_part(i):
+        def step(k):
+            d = distance(k)
+            pltpu.make_async_remote_copy(
+                src_ref=nloc.at[SPAN[i]], dst_ref=nrecv.at[d - 1, SPAN[i]],
+                send_sem=nsend.at[i], recv_sem=nsem.at[i],
+                device_id=panel(d), device_id_type=MESH,
+            ).start()
+
+        each(7, step)
 
     def bank_part(j, carry):
         rows = pl.ds(pl.multiple_of(j * PC, PC), PC)
@@ -82,20 +113,15 @@
         l2 = m * c2 + jnp.log(s) * LOG2E
         for i in range(PR):
             nloc[pl.ds(j * PR + i, 1), :] = l2[:, i * 128 : (i + 1) * 128]
+
+        @pl.when(j == PARTS - 2)
+        def _():
+            pl.semaphore_wait(barrier, 18)
+            send_part(0)
+
         return carry
 
-    def send_part(i):
-        for d in FAR:
-            pltpu.make_async_remote_copy(
-                src_ref=nloc.at[SPAN[i]], dst_ref=nrecv.at[d - 1, SPAN[i]],
-                send_sem=nsend.at[i], recv_sem=nsem.at[i],
-                device_id=panel[d], device_id_type=MESH,
-            ).start()
-
-    lax.fori_loop(0, PARTS - 1, bank_part, 0)
-    pl.semaphore_wait(barrier, len(peers))
-    send_part(0)
-    bank_part(PARTS - 1, 0)
+    lax.fori_loop(0, PARTS, bank_part, 0)
     send_part(1)
 
     loads[-1].wait()
@@ -159,24 +185,32 @@
     sc0[...] = packed(jnp.broadcast_to(peak, (TESTQ, 128)), jnp.broadcast_to(total, (TESTQ, 128)))
     send(sc0, sc0r, 0, 0, sib)
 
-    def pool(tile):
+    mid, outer = 2 - 2 * c, c
+
+    def pool(i, carry):
+        tile = 2 - 2 * c + i * (2 * c - 1)
         lanes = pl.ds(pl.multiple_of(tile * 256, 256), 256)
         out = jnp.dot(wts[...], gal[:, lanes], preferred_element_type=F32)
         work[2 * tile] = out[:, :128]
         work[2 * tile + 1] = out[:, 128:]
 
-    mid, outer = 2 - 2 * c, c
-    pool(2 * (1 - c))
-    send(work.at[pl.ds(4 * (1 - c), 2)], crecv.at[pl.ds(1 - c, 2)], 1, 1, sib)
-    arrived(sc0r, 0)
-    m, t = merged([sc0[...], sc0r[...]], e0)
-    sc1[...] = packed(m, t)
-    for r in (3, 1, 2):
-        device, gp = quad[r]
-        send(sc1.at[pl.ds(gp * 64, 64)], sc1r.at[r - 1], 2, 3, device)
-    pool(1)
-    send(work.at[3 - c], crecv.at[2 * c], 1, 2, sib)
-    pool(2 * c)
+        @pl.when(i == 0)
+        def _():
+            send(work.at[pl.ds(4 * (1 - c), 2)], crecv.at[pl.ds(1 - c, 2)], 1, 1, sib)
+
+        @pl.when(i == 1)
+        def _():
+            send(work.at[3 - c], crecv.at[2 * c], 1, 2, sib)
+            arrived(sc0r, 0)
+            m, t = merged([sc0[...], sc0r[...]], e0)
+            sc1[...] = packed(m, t)
+            for r in (3, 1, 2):
+                device, gp = quad[r]
+                send(sc1.at[pl.ds(gp * 64, 64)], sc1r.at[r - 1], 2, 3, device)
+
+        return carry
+
+    lax.fori_loop(0, 3, pool, 0)
 
     def core_sum(k, b):
         both = e0[0] * work[b] + e0[1] * crecv[k]
@@ -188,19 +222,25 @@
     arrived(crecv.at[mid], 2)
     core_sum(mid, 2 + c)
 
-    for d in FAR + (0,):
+    def quad_in(i):
+        d = distance(i)
         for r in (3, 1, 2):
             device, gp = quad[r]
             send(csum.at[:, gp, (h + d) % 8], s1recv.at[r - 1, d], 3, QUAD_IN + d, device)
 
+    each(8, quad_in)
     arrived(sc1r, 3)
     m, t = merged([sc1[pl.ds(pl.multiple_of(g * 64, 64), 64), :]] + [sc1r[i] for i in range(3)], e1)
     sc2[...] = packed(m, t)
-    for d in FAR:
-        device, hp = ring[d]
-        send(sc2.at[pl.ds(hp * 8, 8)], sc2r.at[d - 1], 4, 4, device)
-
-    for d in FAR + (0,):
+
+    def scalars_in(i):
+        d = distance(i)
+        rows = pl.ds(pl.multiple_of((h + d) % 8 * 8, 8), 8)
+        send(sc2.at[rows], sc2r.at[d - 1], 4, 4, ring(d))
+
+    each(7, scalars_in)
+
+    def quad_sum(d):
         hp = (h + d) % 8
         rows = pl.ds(pl.multiple_of(hp * 8, 8), 8)
         arrived(s1recv.at[:, d], QUAD_IN + d)
@@ -208,15 +248,20 @@
         for i in range(3):
             acc = acc + e1[i + 1, rows, :] * s1recv[i, d]
         s1sum[d] = acc
-        if d:
-            send(s1sum.at[d], s2recv.at[d - 1], 5, 5, ring[d][0])
+
+    def ring_in(i):
+        d = distance(i)
+        quad_sum(d)
+        send(s1sum.at[d], s2recv.at[d - 1], 5, 5, ring(d))
+
+    each(7, ring_in)
+    quad_sum(0)
 
     arrived(sc2r, 4)
     rows8 = pl.ds(pl.multiple_of(h * 8, 8), 8)
     m, t = merged([sc2[rows8, :]] + [sc2r[i] for i in range(7)], e2)
     lsef[g, h] = m * LN2 + jnp.log(t)
-    for d in FAR:
-        send(lsef.at[g, h], lsef.at[g, h], 6, 6, ring[d][0])
+    each(7, lambda i: send(lsef.at[g, h], lsef.at[g, h], 6, 6, ring(distance(i))))
     inv = 1.0 / t
     mine = pl.ds(3 * c, 3)
     arrived(s2recv, 5)
@@ -224,32 +269,33 @@
     for i in range(7):
         acc = acc + e2[i + 1] * s2recv[i]
     final[mine, g, h] = acc * inv
-    for d in FAR:
-        send(final.at[mine, g, h], final.at[mine, g, h], 7, RING_OUT + d, ring[d][0])
-
-    for d in NEAR:
-        hp = (h - d + 8) % 8
-        if d:
-            arrived(s2recv.at[0], RING_OUT + d)
-        piece = final.at[mine, g, hp]
+    piece = final.at[mine, g, h]
+    each(7, lambda i: send(piece, piece, 7, RING_OUT + distance(i), ring(distance(i))))
+
+    def quad_out(d):
+        piece = final.at[mine, g, (h - d + 8) % 8]
         for r in (3, 1, 2):
             send(piece, piece, 8, QUAD_OUT + d, quad[r][0])
-        if d == 6:
-            arrived(sc2r, 6)
-            for r in (3, 1, 2):
-                send(lsef.at[g], lsef.at[g], 9, 7, quad[r][0])
-
-    for d in NEAR:
-        hp = (h - d + 8) % 8
+
+    def ring_out(i):
+        d = distance(6 - i)
+        arrived(s2recv.at[0], RING_OUT + d)
+        quad_out(d)
+
+    quad_out(0)
+    each(7, ring_out)
+    arrived(sc2r, 6)
+    for r in (3, 1, 2):
+        send(lsef.at[g], lsef.at[g], 9, 7, quad[r][0])
+
+    def sibling_out(i):
+        d = distance(7 - i)
         arrived(s1recv.at[:, 0], QUAD_OUT + d)
-        send(final.at[mine, :, hp], final.at[mine, :, hp], 10, 8, sib)
-
-    def store(b, k):
-        lanes = pl.ds(pl.multiple_of(b * 128, 128), 128)
-        return pltpu.make_async_copy(final.at[b], pooled_out.at[:, :, :, lanes], osem.at[k])
-
-    for k in range(3):
-        store(3 * c + k, k).start()
+        piece = final.at[mine, :, (h - d + 8) % 8]
+        send(piece, piece, 10, 8, sib)
+
+    each(8, sibling_out)
+
     arrived(sc1r, 7)
     sub = lax.broadcasted_iota(jnp.int32, (128, 128), 0)
     lane = lax.broadcasted_iota(jnp.int32, (128, 128), 1)
@@ -257,11 +303,6 @@
         tile = lsef[2 * i : 2 * i + 2].reshape(128, 128)
         lse_out[i : i + 1, :] = jnp.sum(jnp.where(sub == lane, tile, 0.0), axis=0, keepdims=True)
     arrived(crecv, 8)
-    for k in range(3):
-        store(3 - 3 * c + k, 3 + k).start()
-    for k in range(3):
-        store(3 * c + k, k).wait()
-        store(3 - 3 * c + k, 3 + k).wait()
 
     for i, block in enumerate(SPAN):
         part = nrecv.at[:, block]
@@ -270,28 +311,31 @@
         pltpu.make_async_copy(ref, ref, ssem.at[stage]).wait()
 
 
-def write(norm, lse, pooled, norm_out, lse_out, pooled_out):
-    norm_out[...] = norm[...]
-    lse_out[...] = lse[...]
-    pooled_out[...] = pooled[...]
+def write(norm, lse, parts, norm_out, lse_out, pooled_out, sem):
+    copies = [
+        pltpu.make_async_copy(parts.at[b], pooled_out.at[:, :, :, pl.ds(b * 128, 128)], sem.at[b])
+        for b in range(6)
+    ]
+    copies.append(pltpu.make_async_copy(norm, norm_out, sem.at[6]))
+    copies.append(pltpu.make_async_copy(lse, lse_out, sem.at[7]))
+    for copy in copies:
+        copy.start()
+    for copy in copies:
+        copy.wait()
 
 
 def body(gallery, bank, test):
     vm = pltpu.VMEM
     dma = pltpu.SemaphoreType.DMA
-    norm, lse, pooled = pl.pallas_call(
+    norm, lse, parts = pl.pallas_call(
         kernel,
         out_shape=(
-            jax.ShapeDtypeStruct((CLIPS // 128, 128), F32),
-            jax.ShapeDtypeStruct((TESTQ // 128, 128), F32),
-            jax.ShapeDtypeStruct((4, 8, 8, D), F32),
+            vm((CLIPS // 128, 128), F32),
+            vm((TESTQ // 128, 128), F32),
+            vm((6, 4, 8, 8, 128), F32),
         ),
         in_specs=[pl.BlockSpec(memory_space=pl.ANY)] * 3,
-        out_specs=(
-            pl.BlockSpec(memory_space=pltpu.VMEM),
-            pl.BlockSpec(memory_space=pltpu.VMEM),
-            pl.BlockSpec(memory_space=pl.ANY),
-        ),
+        out_specs=(pl.BlockSpec(memory_space=pltpu.VMEM),) * 3,
         scratch_shapes=[
             vm((CLIPS, D), BF16),
             vm((BANKQ, D), BF16),
@@ -307,7 +351,6 @@
             vm((3, 8, 3, 8, 128), F32),
             vm((8, 3, 8, 128), F32),
             vm((7, 3, 8, 128), F32),
-            vm((6, 4, 8, 8, 128), F32),
             vm((TESTQ, 128), F32),
             vm((TESTQ, 128), F32),
             vm((TESTQ, 128), F32),
@@ -319,22 +362,23 @@
             vm((4, 64, 128), F32),
             vm((8, 8, 128), F32),
             dma((PARTS + 2,)),
-            dma((6,)),
             dma((2,)),
             dma((33,)),
             dma((2,)),
             dma((11,)),
         ],
         compiler_params=pltpu.CompilerParams(
-            collective_id=0, has_side_effects=True, vmem_limit_bytes=62 * 2**20
+            collective_id=0, has_side_effects=True, vmem_limit_bytes=52 * 2**20
         ),
-    )(gallery, bank, test)
+    )(*(pltpu.with_memory_space_constraint(a, pltpu.HBM) for a in (gallery, bank, test)))
     norm, lse, pooled = pl.pallas_call(
         write,
-        out_shape=tuple(jax.ShapeDtypeStruct(a.shape, F32) for a in (norm, lse, pooled)),
+        out_shape=tuple(jax.ShapeDtypeStruct(s, F32) for s in (norm.shape, lse.shape, (4, 8, 8, D))),
         in_specs=[pl.BlockSpec(memory_space=pltpu.VMEM)] * 3,
-        out_specs=(pl.BlockSpec(memory_space=pltpu.VMEM),) * 3,
-    )(norm, lse, pooled)
+        out_specs=(pl.BlockSpec(memory_space=pl.ANY),) * 3,
+        scratch_shapes=[dma((8,))],
+        compiler_params=pltpu.CompilerParams(vmem_limit_bytes=8 * 2**20),
+    )(*(pltpu.with_memory_space_constraint(a, pltpu.VMEM) for a in (norm, lse, parts)))
     return norm.reshape(CLIPS), lse.reshape(TESTQ), pooled.reshape(TESTQ, D)
 
 

time: 62.2 us -> 58.1 us (0.934)
  Pallas kernels: 61.4 us -> 57.3 us
    pallas_call x2, Pallas kernels: 61.4 us -> 57.3 us  [the longest x1 56.4 us: body(): pl.pallas_call(kernel, out_shape=(vm((CLIPS // 128, 128), F32), vm((TESTQ...]
where the time goes in v3:
time: 58.1 us; the launch traced here: 58 us
  Pallas kernels  57.3 us (99%)
  between operations  0.64 us (1%)
    pallas_call x1, Pallas kernels, body(): pl.pallas_call(kernel, out_shape=(vm((CLIPS // 128, 128), F32), vm((TESTQ...  56.4 us

profile of v3, /device:TPU:1, one launch (start us, length us, event | category | flops | bytes accessed | tf_op | source)
XLA Modules:
  0.0 58.0 jit_solution(9622558568317505702)
XLA Ops:
  0.6 56.4 %shard_map.58 = (f32[32,128]{1,0:T(8,128)S(1)}, f32[2,128]{1,0:T(2,128)S(1)}, f32[6,4,8,8,128]{4,3,2,1,0:T(8,128)S(1)}) custom-call(bf16[4096,768]{1,0:T(8,128)(2,1)} %gallery.1, bf16[512,768]{1,0:T(8,128)(2,1)} %bank.1, bf16[256,768]{1,0:T(8,128)(2,1)} %test.1), custom_call_target="tpu_custom_call" | custom-call | tf_op jit(solution)/shard_map/pallas_call | solution.py:330
  57.0 0.9 %shard_map.59 = (f32[32,128]{1,0:T(8,128)}, f32[2,128]{1,0:T(2,128)}, f32[4,8,8,768]{3,2,1,0:T(8,128)}) custom-call(f32[32,128]{1,0:T(8,128)S(1)} %get-tuple-element.9.norm, f32[2,128]{1,0:T(2,128)S(1)} %get-tuple-element.10.lse, f32[6,4,8,8,128]{4,3,2,1,0:T(8,128)S(1)} %get-tuple-element.11.parts), custom_call_target="tpu_custom_call" | custom-call | tf_op jit(solution)/shard_map/pallas_call | solution.py:374

commit v4 on v3

--- a/solution.py
+++ b/solution.py
@@ -25,7 +25,7 @@
 def kernel(
     gallery, bank, test, norm_out, lse_out, final,
     gal, bnk, tst, raw, wts, nloc, nrecv, n2, work, crecv, csum, s1recv, s1sum, s2recv,
-    sc0, sc0r, sc1, sc1r, sc2, sc2r, lsef, e0, e1, e2,
+    sc0, sc0r, sc1, sc1n, sc1r, sc2, sc2r, lsef, lsen, e0, e1, e2,
     lsem, nsem, rsem, nsend, ssem,
 ):
     me, q = lax.axis_index("gal"), lax.axis_index("qry")
@@ -127,11 +127,11 @@
     loads[-1].wait()
 
     def test_part(j, carry):
-        rows = pl.ds(pl.multiple_of(j * 1024, 1024), 1024)
+        rows = pl.ds(pl.multiple_of(j * 2048, 2048), 2048)
         raw[:, rows] = lax.dot_general(tst[...], gal[rows, :], NT, preferred_element_type=F32)
         return carry
 
-    lax.fori_loop(0, CLIPS // 1024, test_part, 0)
+    lax.fori_loop(0, CLIPS // 2048, test_part, 0)
 
     peak = jnp.full((TESTQ, 128), -jnp.inf, F32)
     for i, block in enumerate(SPAN):
@@ -172,15 +172,31 @@
     def spread(a, lane):
         return jnp.broadcast_to(a[:, lane : lane + 1], a.shape)
 
-    def merged(tiles, scales):
-        ms, ts = [spread(a, 0) for a in tiles], [spread(a, 64) for a in tiles]
-        m = functools.reduce(jnp.maximum, ms)
+    def merged(pairs, scales):
+        m = functools.reduce(jnp.maximum, [mi for mi, _ in pairs])
         t = None
-        for i, (mi, ti) in enumerate(zip(ms, ts)):
+        for i, (mi, ti) in enumerate(pairs):
             e = jnp.exp2(mi - m)
             scales[i] = e
             t = e * ti if t is None else t + e * ti
         return m, t
+
+    def pair(tile):
+        return spread(tile, 0), spread(tile, 64)
+
+    sub = lax.broadcasted_iota(jnp.int32, (64, 128), 0)
+    lane = lax.broadcasted_iota(jnp.int32, (64, 128), 1)
+
+    def narrow(tile):
+        hit = (lane == sub) | (lane == sub + 64)
+        return jnp.broadcast_to(jnp.sum(jnp.where(hit, tile, 0.0), axis=0, keepdims=True), (8, 128))
+
+    def wide(row):
+        def column(shift):
+            x = jnp.where(lane == sub + shift, jnp.broadcast_to(row, (64, 128)), 0.0)
+            return jnp.broadcast_to(jnp.sum(x, axis=1, keepdims=True), (64, 128))
+
+        return column(0), column(64)
 
     sc0[...] = packed(jnp.broadcast_to(peak, (TESTQ, 128)), jnp.broadcast_to(total, (TESTQ, 128)))
     send(sc0, sc0r, 0, 0, sib)
@@ -202,11 +218,13 @@
         def _():
             send(work.at[3 - c], crecv.at[2 * c], 1, 2, sib)
             arrived(sc0r, 0)
-            m, t = merged([sc0[...], sc0r[...]], e0)
+            m, t = merged([pair(sc0[...]), pair(sc0r[...])], e0)
             sc1[...] = packed(m, t)
+            for k in range(4):
+                sc1n[k] = narrow(sc1[k * 64 : (k + 1) * 64, :])
             for r in (3, 1, 2):
                 device, gp = quad[r]
-                send(sc1.at[pl.ds(gp * 64, 64)], sc1r.at[r - 1], 2, 3, device)
+                send(sc1n.at[gp], sc1r.at[r - 1], 2, 3, device)
 
         return carry
 
@@ -230,7 +248,7 @@
 
     each(8, quad_in)
     arrived(sc1r, 3)
-    m, t = merged([sc1[pl.ds(pl.multiple_of(g * 64, 64), 64), :]] + [sc1r[i] for i in range(3)], e1)
+    m, t = merged([pair(sc1[pl.ds(pl.multiple_of(g * 64, 64), 64), :])] + [wide(sc1r[i, :1, :]) for i in range(3)], e1)
     sc2[...] = packed(m, t)
 
     def scalars_in(i):
@@ -259,7 +277,7 @@
 
     arrived(sc2r, 4)
     rows8 = pl.ds(pl.multiple_of(h * 8, 8), 8)
-    m, t = merged([sc2[rows8, :]] + [sc2r[i] for i in range(7)], e2)
+    m, t = merged([pair(sc2[rows8, :])] + [pair(sc2r[i]) for i in range(7)], e2)
     lsef[g, h] = m * LN2 + jnp.log(t)
     each(7, lambda i: send(lsef.at[g, h], lsef.at[g, h], 6, 6, ring(distance(i))))
     inv = 1.0 / t
@@ -285,8 +303,9 @@
     quad_out(0)
     each(7, ring_out)
     arrived(sc2r, 6)
+    lsen[g] = narrow(lsef[g].reshape(64, 128))
     for r in (3, 1, 2):
-        send(lsef.at[g], lsef.at[g], 9, 7, quad[r][0])
+        send(lsen.at[g], lsen.at[g], 9, 7, quad[r][0])
 
     def sibling_out(i):
         d = distance(7 - i)
@@ -297,11 +316,9 @@
     each(8, sibling_out)
 
     arrived(sc1r, 7)
-    sub = lax.broadcasted_iota(jnp.int32, (128, 128), 0)
-    lane = lax.broadcasted_iota(jnp.int32, (128, 128), 1)
     for i in range(2):
-        tile = lsef[2 * i : 2 * i + 2].reshape(128, 128)
-        lse_out[i : i + 1, :] = jnp.sum(jnp.where(sub == lane, tile, 0.0), axis=0, keepdims=True)
+        low = lane[:1] < 64
+        lse_out[i : i + 1, :] = jnp.where(low, lsen[2 * i, :1, :], lsen[2 * i + 1, :1, :])
     arrived(crecv, 8)
 
     for i, block in enumerate(SPAN):
@@ -354,10 +371,12 @@
             vm((TESTQ, 128), F32),
             vm((TESTQ, 128), F32),
             vm((TESTQ, 128), F32),
-            vm((3, 64, 128), F32),
+            vm((4, 8, 128), F32),
+            vm((3, 8, 128), F32),
             vm((64, 128), F32),
             vm((7, 8, 128), F32),
             vm((4, 8, 8, 128), F32),
+            vm((4, 8, 128), F32),
             vm((2, TESTQ, 128), F32),
             vm((4, 64, 128), F32),
             vm((8, 8, 128), F32),

time: 58.1 us -> 57.7 us (level)
  no operation moved by 1% of the time
where the time goes in v4:
time: 57.7 us; the launch traced here: 57.6 us
  Pallas kernels  57 us (99%)
  between operations  0.64 us (1%)
    pallas_call x1, Pallas kernels, body(): pl.pallas_call(kernel, out_shape=(vm((CLIPS // 128, 128), F32), vm((TESTQ...  56 us

profile of v4, /device:TPU:1, one launch (start us, length us, event | category | flops | bytes accessed | tf_op | source)
XLA Modules:
  0.0 57.6 jit_solution(3959188600436276358)
XLA Ops:
  0.6 56.0 %shard_map.58 = (f32[32,128]{1,0:T(8,128)S(1)}, f32[2,128]{1,0:T(2,128)S(1)}, f32[6,4,8,8,128]{4,3,2,1,0:T(8,128)S(1)}) custom-call(bf16[4096,768]{1,0:T(8,128)(2,1)} %gallery.1, bf16[512,768]{1,0:T(8,128)(2,1)} %bank.1, bf16[256,768]{1,0:T(8,128)(2,1)} %test.1), custom_call_target="tpu_custom_call" | custom-call | tf_op jit(solution)/shard_map/pallas_call | solution.py:347
  56.6 0.9 %shard_map.59 = (f32[32,128]{1,0:T(8,128)}, f32[2,128]{1,0:T(2,128)}, f32[4,8,8,768]{3,2,1,0:T(8,128)}) custom-call(f32[32,128]{1,0:T(8,128)S(1)} %get-tuple-element.9.norm, f32[2,128]{1,0:T(2,128)S(1)} %get-tuple-element.10.lse, f32[6,4,8,8,128]{4,3,2,1,0:T(8,128)S(1)} %get-tuple-element.11.parts), custom_call_target="tpu_custom_call" | custom-call | tf_op jit(solution)/shard_map/pallas_call | solution.py:393

commit v5 on v4

--- a/solution.py
+++ b/solution.py
@@ -25,7 +25,7 @@
 def kernel(
     gallery, bank, test, norm_out, lse_out, final,
     gal, bnk, tst, raw, wts, nloc, nrecv, n2, work, crecv, csum, s1recv, s1sum, s2recv,
-    sc0, sc0r, sc1, sc1n, sc1r, sc2, sc2r, lsef, lsen, e0, e1, e2,
+    sc0, sc0r, sc1, sc1n, sc1r, sc2, sc2r, lse_own, lser, lsen, e0, e1, e2,
     lsem, nsem, rsem, nsend, ssem,
 ):
     me, q = lax.axis_index("gal"), lax.axis_index("qry")
@@ -189,12 +189,14 @@
 
     def narrow(tile):
         hit = (lane == sub) | (lane == sub + 64)
-        return jnp.broadcast_to(jnp.sum(jnp.where(hit, tile, 0.0), axis=0, keepdims=True), (8, 128))
-
-    def wide(row):
+        return jnp.sum(jnp.where(hit, tile, 0.0), axis=0, keepdims=True)
+
+    def wide(row, first, count):
+        spot = first + lax.broadcasted_iota(jnp.int32, (count, 128), 0)
+
         def column(shift):
-            x = jnp.where(lane == sub + shift, jnp.broadcast_to(row, (64, 128)), 0.0)
-            return jnp.broadcast_to(jnp.sum(x, axis=1, keepdims=True), (64, 128))
+            x = jnp.where(lane[:count] == spot + shift, jnp.broadcast_to(row, (count, 128)), 0.0)
+            return jnp.broadcast_to(jnp.sum(x, axis=1, keepdims=True), (count, 128))
 
         return column(0), column(64)
 
@@ -248,13 +250,12 @@
 
     each(8, quad_in)
     arrived(sc1r, 3)
-    m, t = merged([pair(sc1[pl.ds(pl.multiple_of(g * 64, 64), 64), :])] + [wide(sc1r[i, :1, :]) for i in range(3)], e1)
-    sc2[...] = packed(m, t)
+    m, t = merged([pair(sc1[pl.ds(pl.multiple_of(g * 64, 64), 64), :])] + [wide(sc1r[i], 0, 64) for i in range(3)], e1)
+    sc2[0] = narrow(packed(m, t))
 
     def scalars_in(i):
         d = distance(i)
-        rows = pl.ds(pl.multiple_of((h + d) % 8 * 8, 8), 8)
-        send(sc2.at[rows], sc2r.at[d - 1], 4, 4, ring(d))
+        send(sc2.at[0], sc2r.at[d - 1], 4, 4, ring(d))
 
     each(7, scalars_in)
 
@@ -276,10 +277,11 @@
     quad_sum(0)
 
     arrived(sc2r, 4)
-    rows8 = pl.ds(pl.multiple_of(h * 8, 8), 8)
-    m, t = merged([pair(sc2[rows8, :])] + [pair(sc2r[i]) for i in range(7)], e2)
-    lsef[g, h] = m * LN2 + jnp.log(t)
-    each(7, lambda i: send(lsef.at[g, h], lsef.at[g, h], 6, 6, ring(distance(i))))
+    m, t = merged([wide(r, h * 8, 8) for r in [sc2[0]] + [sc2r[i] for i in range(7)]], e2)
+    lse = m * LN2 + jnp.log(t)
+    spot = h * 8 + lax.broadcasted_iota(jnp.int32, (8, 128), 0)
+    hit = (lane[:8] == spot) | (lane[:8] == spot + 64)
+    lse_own[0] = jnp.sum(jnp.where(hit, lse, 0.0), axis=0, keepdims=True)
     inv = 1.0 / t
     mine = pl.ds(3 * c, 3)
     arrived(s2recv, 5)
@@ -301,9 +303,18 @@
         quad_out(d)
 
     quad_out(0)
+
+    def lse_out_ring(i):
+        d = distance(i)
+        send(lse_own.at[0], lser.at[d - 1], 6, 6, ring(d))
+
+    each(7, lse_out_ring)
     each(7, ring_out)
-    arrived(sc2r, 6)
-    lsen[g] = narrow(lsef[g].reshape(64, 128))
+    arrived(lser, 6)
+    row = lse_own[0]
+    for i in range(7):
+        row = row + lser[i]
+    lsen[g] = row
     for r in (3, 1, 2):
         send(lsen.at[g], lsen.at[g], 9, 7, quad[r][0])
 
@@ -318,7 +329,7 @@
     arrived(sc1r, 7)
     for i in range(2):
         low = lane[:1] < 64
-        lse_out[i : i + 1, :] = jnp.where(low, lsen[2 * i, :1, :], lsen[2 * i + 1, :1, :])
+        lse_out[i : i + 1, :] = jnp.where(low, lsen[2 * i], lsen[2 * i + 1])
     arrived(crecv, 8)
 
     for i, block in enumerate(SPAN):
@@ -371,12 +382,13 @@
             vm((TESTQ, 128), F32),
             vm((TESTQ, 128), F32),
             vm((TESTQ, 128), F32),
-            vm((4, 8, 128), F32),
-            vm((3, 8, 128), F32),
-            vm((64, 128), F32),
-            vm((7, 8, 128), F32),
-            vm((4, 8, 8, 128), F32),
-            vm((4, 8, 128), F32),
+            vm((4, 1, 128), F32),
+            vm((3, 1, 128), F32),
+            vm((1, 1, 128), F32),
+            vm((7, 1, 128), F32),
+            vm((1, 1, 128), F32),
+            vm((7, 1, 128), F32),
+            vm((4, 1, 128), F32),
             vm((2, TESTQ, 128), F32),
             vm((4, 64, 128), F32),
             vm((8, 8, 128), F32),

time: 57.7 us -> 55.6 us (0.964)
  Pallas kernels: 57 us -> 54.8 us
    pallas_call x1, Pallas kernels: 56 us -> 53.8 us  [body(): pl.pallas_call(kernel, out_shape=(vm((CLIPS // 128, 128), F32), vm((TESTQ...]
where the time goes in v5:
time: 55.6 us; the launch traced here: 55.4 us
  Pallas kernels  54.8 us (99%)
  between operations  0.64 us (1%)
    pallas_call x1, Pallas kernels, body(): pl.pallas_call(kernel, out_shape=(vm((CLIPS // 128, 128), F32), vm((TESTQ...  53.8 us

profile of v5, /device:TPU:1, one launch (start us, length us, event | category | flops | bytes accessed | tf_op | source)
XLA Modules:
  0.0 55.4 jit_solution(13938812794789144033)
XLA Ops:
  0.6 53.8 %shard_map.58 = (f32[32,128]{1,0:T(8,128)S(1)}, f32[2,128]{1,0:T(2,128)S(1)}, f32[6,4,8,8,128]{4,3,2,1,0:T(8,128)S(1)}) custom-call(bf16[4096,768]{1,0:T(8,128)(2,1)} %gallery.1, bf16[512,768]{1,0:T(8,128)(2,1)} %bank.1, bf16[256,768]{1,0:T(8,128)(2,1)} %test.1), custom_call_target="tpu_custom_call" | custom-call | tf_op jit(solution)/shard_map/pallas_call | solution.py:358
  54.5 0.9 %shard_map.59 = (f32[32,128]{1,0:T(8,128)}, f32[2,128]{1,0:T(2,128)}, f32[4,8,8,768]{3,2,1,0:T(8,128)}) custom-call(f32[32,128]{1,0:T(8,128)S(1)} %get-tuple-element.9.norm, f32[2,128]{1,0:T(2,128)S(1)} %get-tuple-element.10.lse, f32[6,4,8,8,128]{4,3,2,1,0:T(8,128)S(1)} %get-tuple-element.11.parts), custom_call_target="tpu_custom_call" | custom-call | tf_op jit(solution)/shard_map/pallas_call | solution.py:405

commit v6 on v5

--- a/solution.py
+++ b/solution.py
@@ -156,13 +156,24 @@
     peak = jnp.max(peak, axis=1, keepdims=True)
     norm_out[...] = n2[...] * LN2
 
+    there = 4 * (1 - c)
+    ahead = pl.ds(pl.multiple_of(there * 128, 512), 256)
+    work[there] = jnp.zeros((TESTQ, 128), F32)
+    work[there + 1] = jnp.zeros((TESTQ, 128), F32)
+
     def weigh(i, total):
-        lanes = pl.ds(pl.multiple_of(i * 128, 128), 128)
-        e = jnp.exp2(raw[:, lanes] - peak)
-        wts[:, lanes] = e.astype(BF16)
-        return total + e
-
-    total = lax.fori_loop(0, CLIPS // 128, weigh, jnp.zeros((TESTQ, 128), F32), unroll=2)
+        for k in range(8):
+            lanes = pl.ds(pl.multiple_of(i * 1024 + k * 128, 128), 128)
+            e = jnp.exp2(raw[:, lanes] - peak)
+            wts[:, lanes] = e.astype(BF16)
+            total = total + e
+        rows = pl.ds(pl.multiple_of(i * 1024, 1024), 1024)
+        out = jnp.dot(wts[:, rows], gal[rows, ahead], preferred_element_type=F32)
+        work[there] += out[:, :128]
+        work[there + 1] += out[:, 128:]
+        return total
+
+    total = lax.fori_loop(0, CLIPS // 1024, weigh, jnp.zeros((TESTQ, 128), F32))
     total = jnp.sum(total, axis=1, keepdims=True)
 
     def packed(m, t):
@@ -202,6 +213,7 @@
 
     sc0[...] = packed(jnp.broadcast_to(peak, (TESTQ, 128)), jnp.broadcast_to(total, (TESTQ, 128)))
     send(sc0, sc0r, 0, 0, sib)
+    send(work.at[pl.ds(there, 2)], crecv.at[pl.ds(1 - c, 2)], 1, 1, sib)
 
     mid, outer = 2 - 2 * c, c
 
@@ -211,10 +223,6 @@
         out = jnp.dot(wts[...], gal[:, lanes], preferred_element_type=F32)
         work[2 * tile] = out[:, :128]
         work[2 * tile + 1] = out[:, 128:]
-
-        @pl.when(i == 0)
-        def _():
-            send(work.at[pl.ds(4 * (1 - c), 2)], crecv.at[pl.ds(1 - c, 2)], 1, 1, sib)
 
         @pl.when(i == 1)
         def _():
@@ -230,7 +238,7 @@
 
         return carry
 
-    lax.fori_loop(0, 3, pool, 0)
+    lax.fori_loop(1, 3, pool, 0)
 
     def core_sum(k, b):
         both = e0[0] * work[b] + e0[1] * crecv[k]

time: 55.6 us -> 57.4 us (1.032)
  Pallas kernels: 54.8 us -> 56.6 us
    pallas_call x1, Pallas kernels: 53.8 us -> 55.7 us  [body(): pl.pallas_call(kernel, out_shape=(vm((CLIPS // 128, 128), F32), vm((TESTQ...]
where the time goes in v6:
time: 57.4 us; the launch traced here: 57.3 us
  Pallas kernels  56.6 us (99%)
  between operations  0.64 us (1%)
    pallas_call x1, Pallas kernels, body(): pl.pallas_call(kernel, out_shape=(vm((CLIPS // 128, 128), F32), vm((TESTQ...  55.7 us

profile of v6, /device:TPU:1, one launch (start us, length us, event | category | flops | bytes accessed | tf_op | source)
XLA Modules:
  0.0 57.3 jit_solution(14883533114570492229)
XLA Ops:
  0.6 55.7 %shard_map.58 = (f32[32,128]{1,0:T(8,128)S(1)}, f32[2,128]{1,0:T(2,128)S(1)}, f32[6,4,8,8,128]{4,3,2,1,0:T(8,128)S(1)}) custom-call(bf16[4096,768]{1,0:T(8,128)(2,1)} %gallery.1, bf16[512,768]{1,0:T(8,128)(2,1)} %bank.1, bf16[256,768]{1,0:T(8,128)(2,1)} %test.1), custom_call_target="tpu_custom_call" | custom-call | tf_op jit(solution)/shard_map/pallas_call | solution.py:366
  56.3 0.9 %shard_map.59 = (f32[32,128]{1,0:T(8,128)}, f32[2,128]{1,0:T(2,128)}, f32[4,8,8,768]{3,2,1,0:T(8,128)}) custom-call(f32[32,128]{1,0:T(8,128)S(1)} %get-tuple-element.9.norm, f32[2,128]{1,0:T(2,128)S(1)} %get-tuple-element.10.lse, f32[6,4,8,8,128]{4,3,2,1,0:T(8,128)S(1)} %get-tuple-element.11.parts), custom_call_target="tpu_custom_call" | custom-call | tf_op jit(solution)/shard_map/pallas_call | solution.py:413
